TPU v7x, 32 devices: a whole 2x2x4 slice. The times are simulated.
32 devices in a mesh: tm: 4 (over y, x), space: 8 (over z, core).
Axes of the slice: x: 2, y: 2, z: 4, core: 2. Of those that a mesh axis runs over, the one named last changes fastest.
Arguments:
- video: bfloat16 [16, 16, 24, 3072], P('tm', 'space'), may hold values from -6 to 6
- w_qkv: bfloat16 [3072, 8, 384], P(None, 'space'), may hold values from -0.109375 to 0.109375
- w_out: bfloat16 [8, 128, 3072], P('space'), may hold values from -0.5 to 0.5
- q_gain: float32 [128], replicated, may hold values from 1 to 8
- k_gain: float32 [128], replicated, may hold values from 1 to 8
- tile_perm: int32 [4, 1536], P('tm'), may hold values from 0 to 1535, as said below
- window: int32 [6, 6], replicated, may hold values from 0 to 5, as said below
Outputs:
- mixed: bfloat16 [4, 1536, 3072], P('tm', 'space')
Inputs may be any that keep to these rules, and one draw needn't show every extreme that they name: `tile_perm`: each row is a permutation of the slots of one frame group in which slots t*256 to t*256 + 255 hold exactly the tokens of tile t; tile t covers frames of the group, rows (t // 3) * 8 onward and columns (t % 3) * 8 onward, 8 and 8 of them. `window`: row t holds 6 different tiles, the first being t.
All inputs are finite; a program needn't handle non-finite values.
Results may differ from a plain program's by a relative error of at most 0.023.
The roundings to bfloat16 on the way count: a program that leaves them out, or rounds other values in their place, can miss the bound.
Values may be sent and summed in bfloat16 or wider, within the bound.
A program may use at most 128 MiB of HBM per device.

v0:
```python
import functools
import math

import jax
import jax.numpy as jnp
from jax import lax
from jax.experimental import pallas as pl
from jax.experimental.pallas import tpu as pltpu
from jax.sharding import PartitionSpec as P

MESH = pl.DeviceIdType.MESH
TT = 4
TH = 8
TW = 8


def fused_kernel(
    n_tm,
    n_z,
    frame,
    x_ref,
    wq_ref,
    wo_ref,
    qg_ref,
    kg_ref,
    perm_ref,
    out_ref,
    xg,
    wall,
    inner_w,
    stage,
    place,
    kv,
    scores,
    attn,
    attn_in,
    part_out,
    part_in,
    own,
    wz_send,
    wz_recv,
    wt_send,
    wt_recv,
    x_send,
    x_recv,
    sib_send,
    sib_recv,
    kv_send,
    kv_recv,
    at_send,
    at_recv,
    pt_send,
    pt_recv,
    wq_send,
    wq_recv,
    wp_send,
    wp_recv,
    qkv_send,
    qkv_recv,
):
    tm = lax.axis_index("tm")
    space = lax.axis_index("space")
    z = space // 2
    core = space % 2
    sibling = z * 2 + 1 - core
    tokens, model = x_ref.shape
    shards = 2 * n_z
    group = shards * tokens
    hd = kv.shape[2] // 4
    quarter = model // n_tm
    inner = jnp.logical_and(z > 0, z < n_z - 1)
    outer = jnp.logical_not(inner)
    end_of = (z - 1) * (n_z - 1)
    inner_of = 1 + z // (n_z - 1)

    def remote(src, dst, send, recv, t, s):
        return pltpu.make_async_remote_copy(
            src_ref=src, dst_ref=dst, send_sem=send, recv_sem=recv,
            device_id=(t, s), device_id_type=MESH,
        )

    def rows_of(index, count):
        return pl.ds(pl.multiple_of(index * count, count), count)

    def w_ring(way, u, zz):
        target = z + 1 if way == 0 else z - 1
        block = wall.at[tm, rows_of(zz, hd)]
        return remote(block, block, wz_send.at[way, u], wz_recv.at[way, u], tm, target * 2 + core)

    def x_ring(way, u, zz, part):
        target = z + 1 if way == 0 else z - 1
        block = xg.at[zz * 2 + core, pl.ds(part * (tokens // 2), tokens // 2)]
        return remote(
            block, block, x_send.at[way, u, part], x_recv.at[way, u, part], tm, target * 2 + core
        )

    def w_peer(k, zz, owner):
        block = wall.at[owner, rows_of(zz, hd)]
        return remote(
            block, block, wt_send.at[k - 1, zz], wt_recv.at[k - 1, zz], (tm + k) % n_tm, space
        )

    def x_sibling(zz, side):
        block = xg.at[zz * 2 + side]
        return remote(block, block, sib_send.at[zz], sib_recv.at[zz], tm, sibling)

    def kv_copy(way, zz):
        target = tm - 1 if way == 0 else tm + 1
        rows = rows_of(zz, 2 * tokens)
        return remote(
            kv.at[0, rows, pl.ds(hd, 2 * hd)],
            kv.at[2 - way, rows, pl.ds(hd, 2 * hd)],
            kv_send.at[way, zz],
            kv_recv.at[way, zz],
            target,
            space,
        )

    def wq_inward():
        rows = rows_of(tm, quarter)
        return remote(
            wq_ref.at[rows], inner_w.at[rows], wq_send, wq_recv, tm, inner_of * 2 + core
        )

    beside = tm + 1 - 2 * (tm % 2)
    across = (tm + n_tm // 2) % n_tm

    def wq_peer(k, owner):
        block = inner_w.at[rows_of(owner, quarter)]
        target = beside if k == 0 else across
        return remote(block, block, wp_send.at[k], wp_recv.at[k], target, space)

    def qkv_outward(zz):
        return remote(
            stage,
            kv.at[0, rows_of(zz, 2 * tokens), pl.ds(0, 3 * hd)],
            qkv_send,
            qkv_recv,
            tm,
            end_of * 2 + core,
        )

    def attn_copy(zz):
        return remote(
            attn.at[zz], attn_in.at[z], at_send.at[zz], at_recv.at[z], tm, zz * 2 + core
        )

    def attn_arrival(zz):
        return remote(
            attn.at[zz], attn_in.at[zz], at_send.at[zz], at_recv.at[zz], tm, zz * 2 + core
        )

    def part_copy(j):
        return remote(
            part_out.at[j], part_in.at[j], pt_send.at[j], pt_recv.at[j], tm, sibling
        )

    barrier = pltpu.get_barrier_semaphore()
    for k in range(1, n_z):
        pl.semaphore_signal(
            barrier, inc=1, device_id=(tm, (z + k) % n_z * 2 + core), device_id_type=MESH
        )
    for k in range(1, n_tm):
        pl.semaphore_signal(barrier, inc=1, device_id=((tm + k) % n_tm, space), device_id_type=MESH)
    pl.semaphore_signal(barrier, inc=1, device_id=(tm, sibling), device_id_type=MESH)
    for j in range(n_tm):
        wall[j, rows_of(z, hd), :] = wo_ref[:, j * quarter : (j + 1) * quarter]
    xg[space] = x_ref[...]
    kv[0, :, 3 * hd :] = jnp.ones((group, hd), jnp.bfloat16)
    pl.semaphore_wait(barrier, n_z - 1 + n_tm - 1 + 1)

    def norm(value, gain):
        scaled = value * lax.rsqrt(jnp.mean(value * value, axis=-1, keepdims=True) + 1e-06)
        return (scaled * gain).astype(jnp.bfloat16)

    def project(zz, weights):
        both = xg[rows_of(zz, 2)].reshape(2 * tokens, model)
        qkv = jnp.dot(both, weights[...], preferred_element_type=jnp.float32)
        qkv = qkv.astype(jnp.bfloat16)
        query = norm(qkv[:, :hd].astype(jnp.float32), qg_ref[...])
        key = norm(qkv[:, hd : 2 * hd].astype(jnp.float32), kg_ref[...])
        return jnp.concatenate([query, key, qkv[:, 2 * hd :]], axis=1)

    def inside(zz):
        return jnp.logical_and(zz >= 0, zz < n_z)

    def forwards_w(way):
        return z < n_z - 1 if way == 0 else z > 0

    def spread_w(u):
        for way in (0, 1):
            zz = z - u if way == 0 else z + u
            live = inside(zz)

            @pl.when(jnp.logical_and(live, u > 0))
            def _():
                w_ring(way, u - 1, zz).wait_recv()

            @pl.when(jnp.logical_and(live, forwards_w(way)))
            def _():
                w_ring(way, u, zz).start()

            @pl.when(jnp.logical_and(jnp.logical_and(live, outer), u > 0))
            def _():
                for k in range(1, n_tm):
                    w_peer(k, zz, tm).start()

    def step(u, carry):
        def arrive(part):
            for way in (0, 1):
                zz = z - u if way == 0 else z + u

                @pl.when(jnp.logical_and(inside(zz), jnp.logical_and(u > 0, u < n_z - 1)))
                def _():
                    x_ring(way, u - 1, zz, part).wait_recv()

                going = jnp.logical_and(jnp.logical_or(inner, u >= part), u < n_z - 2)

                @pl.when(jnp.logical_and(jnp.logical_and(inside(zz), going), forwards_w(way)))
                def _():
                    x_ring(way, u, zz, part).start()

        arrive(0)

        @pl.when(jnp.logical_and(inner, u == 1))
        def _():
            wq_inward().wait_recv()
            for k in (0, 1):
                wq_peer(k, tm).start()

        arrive(1)

        @pl.when(jnp.logical_and(inner, u == 1))
        def _():
            wq_peer(0, beside).wait_recv()
            wq_peer(2, beside).start()

        for way in (0, 1):
            zz = z - u if way == 0 else z + u
            live = jnp.logical_and(inside(zz), u < n_z - 1)
            fresh = live if way == 0 else jnp.logical_and(live, u > 0)

            @pl.when(fresh)
            def _():
                x_sibling(zz, core).start()

        @pl.when(outer)
        def _():
            spread_w(u)

        def item(way, carry):
            zz = z - u + way * 2 * u
            fresh = jnp.logical_and(inside(zz), way * (1 - jnp.minimum(u, 1)) == 0)

            @pl.when(jnp.logical_and(fresh, u < n_z - 1))
            def _():
                x_sibling(zz, 1 - core).wait_recv()
                kv[0, rows_of(zz, 2 * tokens), 0 : 3 * hd] = project(zz, wq_ref)

            @pl.when(jnp.logical_and(fresh, u == n_z - 1))
            def _():
                qkv_outward(zz).wait_recv()

            @pl.when(jnp.logical_and(fresh, tm > 0))
            def _():
                kv_copy(0, zz).start()

            @pl.when(jnp.logical_and(fresh, tm < n_tm - 1))
            def _():
                kv_copy(1, zz).start()

            return carry

        lax.fori_loop(0, 2, item, 0)

        for way in (0, 1):

            @pl.when(jnp.logical_and(jnp.logical_and(outer, u == 0), forwards_w(way)))
            def _():
                x_ring(way, u, z, 0).wait_send()
                wq_inward().start()
                wq_inward().wait_send()
                x_ring(way, u, z, 1).start()

        @pl.when(inner)
        def _():
            spread_w(u)

        @pl.when(jnp.logical_and(inner, u == n_z - 2))
        def _():
            wq_peer(1, across).wait_recv()
            wq_peer(2, (beside + n_tm // 2) % n_tm).wait_recv()
            far = n_z - 1 - end_of
            stage[...] = project(far, inner_w)
            qkv_outward(far).start()

        return carry

    token = perm_ref[...].astype(jnp.float32)
    rows_here, cols, plane = frame

    def whole(value, by):
        return jnp.floor((value + 0.5) * (1.0 / by))

    at_frame = whole(token, plane)
    token = token - at_frame * plane
    row = whole(token, cols)
    col = token - row * cols
    shard = whole(row, rows_here)
    pos = shard * tokens + (at_frame * rows_here + row - shard * rows_here) * cols + col
    for i in range(group // hd):
        block = jnp.broadcast_to(pos[:, i * hd : (i + 1) * hd], (hd, hd))
        place[i * hd : (i + 1) * hd, :] = block.T

    lax.fori_loop(0, n_z, step, 0)

    def others(body):
        for k in range(1, n_z):
            body((z + k) % n_z)

    def weights_out(zz):
        for k in range(1, n_tm):
            w_peer(k, zz, tm).start()

    @pl.when(inner)
    def _():
        others(weights_out)

    for way in (0, 1):
        here = 2 - way
        live = tm < n_tm - 1 if way == 0 else tm > 0

        @pl.when(live)
        def _():
            kv[here, :, 3 * hd :] = jnp.ones((group, hd), jnp.bfloat16)

            for zz in range(n_z):
                kv_copy(way, zz).wait_recv()

        @pl.when(jnp.logical_not(live))
        def _():
            kv[here, :, hd : 2 * hd] = kv[0, :, hd : 2 * hd]
            kv[here, :, 2 * hd :] = jnp.zeros((group, 2 * hd), jnp.bfloat16)

    factor = math.log2(math.e) * hd**-0.5
    block_rows = 2 * tokens

    def attend_block(i, carry):
        zz = (z + 1 + i) % n_z
        pos = place[rows_of(zz, block_rows), :]
        lanes = lax.broadcasted_iota(jnp.int32, (block_rows, hd), 1).astype(jnp.float32)
        picks = [jnp.where(pos - i * hd == lanes, 1.0, 0.0) for i in range(group // hd)]
        pick = jnp.concatenate([p.astype(jnp.bfloat16) for p in picks], axis=1)
        query = jnp.dot(pick, kv[0, :, 0:hd], preferred_element_type=jnp.float32)
        query = query.astype(jnp.bfloat16)
        highest = None
        for part in range(3):
            score = lax.dot_general(
                query,
                kv[part, :, hd : 2 * hd],
                (((1,), (1,)), ((), ())),
                preferred_element_type=jnp.float32,
            )
            scores[part] = score
            top = jnp.max(score, axis=-1, keepdims=True)
            highest = top if highest is None else jnp.maximum(highest, top)
        total = jnp.zeros((block_rows, 2 * hd), jnp.float32)
        for part in range(3):
            weights = jnp.exp2((scores[part] - highest) * factor).astype(jnp.bfloat16)
            total += jnp.dot(weights, kv[part, :, 2 * hd :], preferred_element_type=jnp.float32)
        result = (total[:, :hd] / total[:, hd:]).astype(jnp.bfloat16)

        @pl.when(zz == z)
        def _():
            attn_in[z] = result

        @pl.when(zz != z)
        def _():
            attn[zz] = result
            attn_copy(zz).start()

        return carry

    lax.fori_loop(0, n_z, attend_block, 0)

    def weights_in(zz):
        for k in range(1, n_tm):
            w_peer(k, zz, (tm + n_tm - k) % n_tm).wait_recv()

    others(weights_in)
    others(lambda zz: attn_arrival(zz).wait_recv())

    def heads(side):
        rows = rows_of(side, tokens)
        return jnp.concatenate([attn_in[zz, rows, :] for zz in range(n_z)], axis=1)

    left = jnp.concatenate([heads(1 - core), heads(core)], axis=0)
    for j in range(n_tm):
        both = jnp.dot(left, wall[j], preferred_element_type=jnp.float32)
        part_out[j] = both[:tokens].astype(jnp.bfloat16)
        part_copy(j).start()
        own[j] = both[tokens:]
    for j in range(n_tm):
        part_copy(j).wait_recv()
        total = own[j] + part_in[j].astype(jnp.float32)
        out_ref[:, j * quarter : (j + 1) * quarter] = total.astype(jnp.bfloat16)

    for j in range(n_tm):
        part_copy(j).wait_send()

    def sent(zz):
        attn_copy(zz).wait_send()
        for k in range(1, n_tm):
            w_peer(k, zz, tm).wait_send()

    others(sent)

    for zz in range(n_z):

        @pl.when(tm > 0)
        def _():
            kv_copy(0, zz).wait_send()

        @pl.when(tm < n_tm - 1)
        def _():
            kv_copy(1, zz).wait_send()

        far = jnp.logical_and(outer, zz == n_z - 1 - z)

        @pl.when(jnp.logical_not(far))
        def _():
            x_sibling(zz, core).wait_send()

    for u in range(n_z - 1):
        for way in (0, 1):
            zz = z - u if way == 0 else z + u

            @pl.when(jnp.logical_and(inside(zz), forwards_w(way)))
            def _():
                w_ring(way, u, zz).wait_send()

            for part in (0, 1):
                live = u < n_z - 2
                if u == 0 and part == 0:
                    live = inner

                @pl.when(jnp.logical_and(jnp.logical_and(live, inside(zz)), forwards_w(way)))
                def _():
                    x_ring(way, u, zz, part).wait_send()

    @pl.when(inner)
    def _():
        wq_peer(0, tm).wait_send()
        wq_peer(1, tm).wait_send()
        wq_peer(2, beside).wait_send()
        qkv_outward(n_z - 1 - end_of).wait_send()


def fused(n_tm, n_z, frame, x, wq, wo, q_gain, k_gain, perm):
    tokens, model = x.shape
    hd = wo.shape[0]
    shards = 2 * n_z
    group = shards * tokens
    bf = jnp.bfloat16
    dma = pltpu.SemaphoreType.DMA
    vmem = pl.BlockSpec(memory_space=pltpu.VMEM)
    return pl.pallas_call(
        functools.partial(fused_kernel, n_tm, n_z, frame),
        out_shape=jax.ShapeDtypeStruct((tokens, model), bf),
        in_specs=[vmem] * 6,
        out_specs=vmem,
        scratch_shapes=[
            pltpu.VMEM((shards, tokens, model), bf),
            pltpu.VMEM((n_tm, n_z * hd, model // n_tm), bf),
            pltpu.VMEM((model, 3 * hd), bf),
            pltpu.VMEM((2 * tokens, 3 * hd), bf),
            pltpu.VMEM((group, hd), jnp.float32),
            pltpu.VMEM((3, group, 4 * hd), bf),
            pltpu.VMEM((3, 2 * tokens, group), jnp.float32),
            pltpu.VMEM((n_z, 2 * tokens, hd), bf),
            pltpu.VMEM((n_z, 2 * tokens, hd), bf),
            pltpu.VMEM((n_tm, tokens, model // n_tm), bf),
            pltpu.VMEM((n_tm, tokens, model // n_tm), bf),
            pltpu.VMEM((n_tm, tokens, model // n_tm), jnp.float32),
            dma((2, n_z)),
            dma((2, n_z)),
            dma((n_tm - 1, n_z)),
            dma((n_tm - 1, n_z)),
            dma((2, n_z, 2)),
            dma((2, n_z, 2)),
            dma((n_z,)),
            dma((n_z,)),
            dma((2, n_z)),
            dma((2, n_z)),
            dma((n_z,)),
            dma((n_z,)),
            dma((n_tm,)),
            dma((n_tm,)),
            dma,
            dma,
            dma((n_tm - 1,)),
            dma((n_tm - 1,)),
            dma,
            dma,
        ],
        compiler_params=pltpu.CompilerParams(
            collective_id=0, has_side_effects=True, vmem_limit_bytes=56 * 1024 * 1024
        ),
    )(x, wq, wo, q_gain, k_gain, perm)


def whole_window(video, w_qkv, w_out, q_gain, k_gain, tile_perm):
    frames, rows_here, cols, model = video.shape
    n_tm = lax.axis_size("tm")
    n_space = lax.axis_size("space")
    hd = w_out.shape[1]
    tokens = frames * rows_here * cols
    mixed = fused(
        n_tm,
        n_space // 2,
        (rows_here, cols, rows_here * n_space * cols),
        video.reshape(tokens, model),
        w_qkv.reshape(model, 3 * hd),
        w_out.reshape(hd, model),
        q_gain.reshape(1, hd),
        k_gain.reshape(1, hd),
        tile_perm,
    )
    return mixed[None]


def extended(cells, sides, width):
    for axis, dim in sides:
        count = lax.axis_size(axis)
        ends = count - 1
        head = lax.slice_in_dim(cells, 0, width, axis=dim)
        tail = lax.slice_in_dim(cells, cells.shape[dim] - width, cells.shape[dim], axis=dim)
        cells = jnp.concatenate(
            [
                lax.ppermute(tail, axis, [(i, (i + 1) % count) for i in range(ends)]),
                cells,
                lax.ppermute(head, axis, [((i + 1) % count, i) for i in range(ends)]),
            ],
            axis=dim,
        )
    return cells


def head_norm(values, gain):
    wide = values.astype(jnp.float32)
    scaled = wide * lax.rsqrt(jnp.mean(wide * wide, axis=-1, keepdims=True) + 1e-06)
    return (scaled * gain).astype(jnp.bfloat16)


def attend(queries, chosen, valid):
    heads_here = queries.shape[1]
    head_dim = queries.shape[2]
    span = chosen.shape[1] * chosen.shape[2]
    keys = chosen[:, :, :, :, 0, :].reshape(-1, heads_here, head_dim)
    values = chosen[:, :, :, :, 1, :].reshape(-1, heads_here, head_dim)
    scores = jnp.einsum(
        "qhd,khd->hqk", queries, keys, preferred_element_type=jnp.float32
    ) * head_dim ** (-0.5)
    live = jnp.repeat(valid, span)
    scores = jnp.where(live[None, None, :], scores, -jnp.inf)
    highest = jnp.max(scores, axis=-1, keepdims=True)
    weights = jnp.exp(scores - highest)
    probs = (weights / jnp.sum(weights, axis=-1, keepdims=True)).astype(jnp.bfloat16)
    result = jnp.einsum("hqk,khd->qhd", probs, values, preferred_element_type=jnp.float32)
    return result.astype(jnp.bfloat16)


def per_device(video, w_qkv, w_out, q_gain, k_gain, tile_perm, window):
    tiles = video.shape[0] * video.shape[1] * lax.axis_size("space") * video.shape[2] // (TT * TH * TW)
    sized = lax.axis_size("tm") == 4 and lax.axis_size("space") == 8
    if window.shape[1] == tiles and w_qkv.shape[1] == 1 and sized:
        return whole_window(video, w_qkv, w_out, q_gain, k_gain, tile_perm)
    frames_here = video.shape[0]
    cols_here = video.shape[2]
    model_dim = video.shape[3]
    heads_here = w_qkv.shape[1]
    head_dim = w_out.shape[1]
    flat_w = w_qkv.reshape(model_dim, heads_here * 3 * head_dim)
    qkv = jnp.einsum(
        "frwd,dc->frwc",
        lax.all_gather(video, "space", axis=1, tiled=True),
        flat_w,
        preferred_element_type=jnp.float32,
    ).astype(jnp.bfloat16)
    group_tokens = frames_here * qkv.shape[1] * cols_here
    qkv = qkv.reshape(group_tokens, heads_here, 3, head_dim)
    ordered = jnp.take(qkv, tile_perm[0], axis=0)
    queries = head_norm(ordered[:, :, 0, :], q_gain)
    keys = head_norm(ordered[:, :, 1, :], k_gain)
    pairs = jnp.stack([keys, ordered[:, :, 2, :]], axis=2)
    beside_all = extended(pairs[None], (("tm", 0),), 1)
    tile_tokens = TT * TH * TW
    tile_count = group_tokens // tile_tokens
    beside_all = beside_all.reshape(3, tile_count, tile_tokens, heads_here, 2, head_dim)
    position = lax.axis_index("tm")
    valid = jnp.stack([position > 0, position >= 0, position < lax.axis_size("tm") - 1])
    query_tiles = queries.reshape(tile_count, tile_tokens, heads_here, head_dim)

    def one_tile(item):
        block, picks = item
        return attend(block, jnp.take(beside_all, picks, axis=1), valid)

    attn = lax.map(one_tile, (query_tiles, window)).reshape(group_tokens, heads_here, head_dim)
    flat_attn = attn.reshape(group_tokens, heads_here * head_dim)
    flat_out = w_out.reshape(heads_here * head_dim, model_dim)
    product = jnp.dot(flat_attn, flat_out, preferred_element_type=jnp.float32)
    summed = lax.psum_scatter(
        lax.optimization_barrier(product.astype(jnp.bfloat16))
        .astype(jnp.float32)
        .astype(jnp.bfloat16),
        "space",
        scatter_dimension=0,
        tiled=True,
    )
    return summed[None]


def solution(mesh):
    in_specs = (
        P("tm", "space", None, None),
        P(None, "space", None),
        P("space", None, None),
        P(),
        P(),
        P("tm", None),
        P(),
    )
    out_specs = P("tm", "space", None)
    return jax.shard_map(
        per_device, mesh=mesh, in_specs=in_specs, out_specs=out_specs, check_vma=False
    )
```

profile of v0, /device:TPU:5, one launch (start us, length us, event | category | flops | bytes accessed | tf_op | source)
XLA Modules:
  0.0 129.2 jit_solution(14094603990774543287)
XLA Ops:
  0.0 126.8 %shard_map.64 = bf16[192,3072]{1,0:T(8,128)(2,1)} custom-call(bf16[192,3072]{1,0:T(8,128)(2,1)} %bitcast.8, bf16[3072,384]{1,0:T(8,128)(2,1)} %bitcast.7, bf16[128,3072]{1,0:T(8,128)(2,1)} %bitcast.9, f32[1,128]{1,0:T(1,128)} %bitcast.10, f32[1,128]{1,0:T(1,128)} %bitcast.11, s32[1,1536]{1,0:T(1,128)} %perm_ref.1), custom_call_target="tpu_custom_call" | custom-call | tf_op jit(solution)/shard_map/pallas_call | solution.py:467
  126.8 2.4 %copy.8 = bf16[1,192,3072]{2,1,0:T(8,128)(2,1)} copy(bf16[1,192,3072]{2,1,0:T(8,128)(2,1)} %bitcast.6) | data formatting | bytes 2359296
where the time goes:
time: 129 us
  Pallas kernels  127 us (98%)
  local copies, waits for them, and re-layouts  2.36 us (2%)
    pallas_call x1, Pallas kernels, fused(): pl.pallas_call(functools.partial(fused_kernel, n_tm, n_z, frame), out_sha...  127 us

commit v1 on v0

--- a/solution.py
+++ b/solution.py
@@ -100,18 +100,18 @@
             block, block, wt_send.at[k - 1, zz], wt_recv.at[k - 1, zz], (tm + k) % n_tm, space
         )
 
-    def x_sibling(zz, side):
-        block = xg.at[zz * 2 + side]
-        return remote(block, block, sib_send.at[zz], sib_recv.at[zz], tm, sibling)
-
-    def kv_copy(way, zz):
+    def x_sibling(zz, side, part):
+        block = xg.at[zz * 2 + side, pl.ds(part * (tokens // 2), tokens // 2)]
+        return remote(block, block, sib_send.at[zz, part], sib_recv.at[zz, part], tm, sibling)
+
+    def kv_copy(way, zz, side):
         target = tm - 1 if way == 0 else tm + 1
-        rows = rows_of(zz, 2 * tokens)
+        rows = rows_of(zz * 2 + side, tokens)
         return remote(
             kv.at[0, rows, pl.ds(hd, 2 * hd)],
             kv.at[2 - way, rows, pl.ds(hd, 2 * hd)],
-            kv_send.at[way, zz],
-            kv_recv.at[way, zz],
+            kv_send.at[way, zz, side],
+            kv_recv.at[way, zz, side],
             target,
             space,
         )
@@ -130,12 +130,13 @@
         target = beside if k == 0 else across
         return remote(block, block, wp_send.at[k], wp_recv.at[k], target, space)
 
-    def qkv_outward(zz):
-        return remote(
-            stage,
-            kv.at[0, rows_of(zz, 2 * tokens), pl.ds(0, 3 * hd)],
-            qkv_send,
-            qkv_recv,
+    def qkv_outward(zz, turn):
+        side = core + turn * (1 - 2 * core)
+        return remote(
+            stage.at[turn],
+            kv.at[0, rows_of(zz * 2 + side, tokens), pl.ds(0, 3 * hd)],
+            qkv_send.at[turn],
+            qkv_recv.at[turn],
             tm,
             end_of * 2 + core,
         )
@@ -173,9 +174,8 @@
         scaled = value * lax.rsqrt(jnp.mean(value * value, axis=-1, keepdims=True) + 1e-06)
         return (scaled * gain).astype(jnp.bfloat16)
 
-    def project(zz, weights):
-        both = xg[rows_of(zz, 2)].reshape(2 * tokens, model)
-        qkv = jnp.dot(both, weights[...], preferred_element_type=jnp.float32)
+    def project(x, weights):
+        qkv = jnp.dot(x, weights[...], preferred_element_type=jnp.float32)
         qkv = qkv.astype(jnp.bfloat16)
         query = norm(qkv[:, :hd].astype(jnp.float32), qg_ref[...])
         key = norm(qkv[:, hd : 2 * hd].astype(jnp.float32), kg_ref[...])
@@ -220,6 +220,13 @@
                 def _():
                     x_ring(way, u, zz, part).start()
 
+                live = jnp.logical_and(inside(zz), u < n_z - 1)
+                fresh = live if way == 0 else jnp.logical_and(live, u > 0)
+
+                @pl.when(fresh)
+                def _():
+                    x_sibling(zz, core, part).start()
+
         arrive(0)
 
         @pl.when(jnp.logical_and(inner, u == 1))
@@ -235,14 +242,26 @@
             wq_peer(0, beside).wait_recv()
             wq_peer(2, beside).start()
 
-        for way in (0, 1):
-            zz = z - u if way == 0 else z + u
-            live = jnp.logical_and(inside(zz), u < n_z - 1)
-            fresh = live if way == 0 else jnp.logical_and(live, u > 0)
-
-            @pl.when(fresh)
-            def _():
-                x_sibling(zz, core).start()
+        last = jnp.logical_and(inner, u == n_z - 2)
+
+        @pl.when(last)
+        def _():
+            wq_peer(1, across).wait_recv()
+            wq_peer(2, (beside + n_tm // 2) % n_tm).wait_recv()
+            far = n_z - 1 - end_of
+
+            def send(turn, carry):
+                @pl.when(turn == 1)
+                def _():
+                    for part in (0, 1):
+                        x_sibling(far, 1 - core, part).wait_recv()
+
+                slot = far * 2 + core + turn * (1 - 2 * core)
+                stage[turn] = project(xg[slot], inner_w)
+                qkv_outward(far, turn).start()
+                return carry
+
+            lax.fori_loop(0, 2, send, 0)
 
         @pl.when(outer)
         def _():
@@ -254,20 +273,28 @@
 
             @pl.when(jnp.logical_and(fresh, u < n_z - 1))
             def _():
-                x_sibling(zz, 1 - core).wait_recv()
-                kv[0, rows_of(zz, 2 * tokens), 0 : 3 * hd] = project(zz, wq_ref)
-
-            @pl.when(jnp.logical_and(fresh, u == n_z - 1))
-            def _():
-                qkv_outward(zz).wait_recv()
-
-            @pl.when(jnp.logical_and(fresh, tm > 0))
-            def _():
-                kv_copy(0, zz).start()
-
-            @pl.when(jnp.logical_and(fresh, tm < n_tm - 1))
-            def _():
-                kv_copy(1, zz).start()
+                @pl.when(jnp.logical_not(last))
+                def _():
+                    for part in (0, 1):
+                        x_sibling(zz, 1 - core, part).wait_recv()
+
+                both = xg[rows_of(zz, 2)].reshape(2 * tokens, model)
+                kv[0, rows_of(zz, 2 * tokens), 0 : 3 * hd] = project(both, wq_ref)
+
+            for turn in (0, 1):
+                side = core + turn * (1 - 2 * core)
+
+                @pl.when(jnp.logical_and(fresh, u == n_z - 1))
+                def _():
+                    qkv_outward(zz, turn).wait_recv()
+
+                @pl.when(jnp.logical_and(fresh, tm > 0))
+                def _():
+                    kv_copy(0, zz, side).start()
+
+                @pl.when(jnp.logical_and(fresh, tm < n_tm - 1))
+                def _():
+                    kv_copy(1, zz, side).start()
 
             return carry
 
@@ -285,14 +312,6 @@
         @pl.when(inner)
         def _():
             spread_w(u)
-
-        @pl.when(jnp.logical_and(inner, u == n_z - 2))
-        def _():
-            wq_peer(1, across).wait_recv()
-            wq_peer(2, (beside + n_tm // 2) % n_tm).wait_recv()
-            far = n_z - 1 - end_of
-            stage[...] = project(far, inner_w)
-            qkv_outward(far).start()
 
         return carry
 
@@ -335,7 +354,8 @@
             kv[here, :, 3 * hd :] = jnp.ones((group, hd), jnp.bfloat16)
 
             for zz in range(n_z):
-                kv_copy(way, zz).wait_recv()
+                for side in (0, 1):
+                    kv_copy(way, zz, side).wait_recv()
 
         @pl.when(jnp.logical_not(live))
         def _():
@@ -419,17 +439,20 @@
 
         @pl.when(tm > 0)
         def _():
-            kv_copy(0, zz).wait_send()
+            for side in (0, 1):
+                kv_copy(0, zz, side).wait_send()
 
         @pl.when(tm < n_tm - 1)
         def _():
-            kv_copy(1, zz).wait_send()
+            for side in (0, 1):
+                kv_copy(1, zz, side).wait_send()
 
         far = jnp.logical_and(outer, zz == n_z - 1 - z)
 
         @pl.when(jnp.logical_not(far))
         def _():
-            x_sibling(zz, core).wait_send()
+            for part in (0, 1):
+                x_sibling(zz, core, part).wait_send()
 
     for u in range(n_z - 1):
         for way in (0, 1):
@@ -453,7 +476,8 @@
         wq_peer(0, tm).wait_send()
         wq_peer(1, tm).wait_send()
         wq_peer(2, beside).wait_send()
-        qkv_outward(n_z - 1 - end_of).wait_send()
+        for turn in (0, 1):
+            qkv_outward(n_z - 1 - end_of, turn).wait_send()
 
 
 def fused(n_tm, n_z, frame, x, wq, wo, q_gain, k_gain, perm):
@@ -473,7 +497,7 @@
             pltpu.VMEM((shards, tokens, model), bf),
             pltpu.VMEM((n_tm, n_z * hd, model // n_tm), bf),
             pltpu.VMEM((model, 3 * hd), bf),
-            pltpu.VMEM((2 * tokens, 3 * hd), bf),
+            pltpu.VMEM((2, tokens, 3 * hd), bf),
             pltpu.VMEM((group, hd), jnp.float32),
             pltpu.VMEM((3, group, 4 * hd), bf),
             pltpu.VMEM((3, 2 * tokens, group), jnp.float32),
@@ -488,10 +512,10 @@
             dma((n_tm - 1, n_z)),
             dma((2, n_z, 2)),
             dma((2, n_z, 2)),
-            dma((n_z,)),
-            dma((n_z,)),
-            dma((2, n_z)),
-            dma((2, n_z)),
+            dma((n_z, 2)),
+            dma((n_z, 2)),
+            dma((2, n_z, 2)),
+            dma((2, n_z, 2)),
             dma((n_z,)),
             dma((n_z,)),
             dma((n_tm,)),
@@ -500,8 +524,8 @@
             dma,
             dma((n_tm - 1,)),
             dma((n_tm - 1,)),
-            dma,
-            dma,
+            dma((2,)),
+            dma((2,)),
         ],
         compiler_params=pltpu.CompilerParams(
             collective_id=0, has_side_effects=True, vmem_limit_bytes=56 * 1024 * 1024

time: 129 us -> 130 us (level)
  no operation moved by 1% of the time
where the time goes in v1:
time: 130 us; the launch traced here: 129 us
  Pallas kernels  127 us (98%)
  local copies, waits for them, and re-layouts  2.36 us (2%)
    pallas_call x1, Pallas kernels, fused(): pl.pallas_call(functools.partial(fused_kernel, n_tm, n_z, frame), out_sha...  127 us

profile of v1, /device:TPU:5, one launch (start us, length us, event | category | flops | bytes accessed | tf_op | source)
XLA Modules:
  0.0 129.5 jit_solution(694018639010885126)
XLA Ops:
  0.0 127.1 %shard_map.64 = bf16[192,3072]{1,0:T(8,128)(2,1)} custom-call(bf16[192,3072]{1,0:T(8,128)(2,1)} %bitcast.8, bf16[3072,384]{1,0:T(8,128)(2,1)} %bitcast.7, bf16[128,3072]{1,0:T(8,128)(2,1)} %bitcast.9, f32[1,128]{1,0:T(1,128)} %bitcast.10, f32[1,128]{1,0:T(1,128)} %bitcast.11, s32[1,1536]{1,0:T(1,128)} %perm_ref.1), custom_call_target="tpu_custom_call" | custom-call | tf_op jit(solution)/shard_map/pallas_call | solution.py:491
  127.1 2.4 %copy.8 = bf16[1,192,3072]{2,1,0:T(8,128)(2,1)} copy(bf16[1,192,3072]{2,1,0:T(8,128)(2,1)} %bitcast.6) | data formatting | bytes 2359296

commit v2 on v1

--- a/solution.py
+++ b/solution.py
@@ -200,7 +200,7 @@
             def _():
                 w_ring(way, u, zz).start()
 
-            @pl.when(jnp.logical_and(jnp.logical_and(live, outer), u > 0))
+            @pl.when(jnp.logical_and(live, u > 0))
             def _():
                 for k in range(1, n_tm):
                     w_peer(k, zz, tm).start()
@@ -336,14 +336,6 @@
     def others(body):
         for k in range(1, n_z):
             body((z + k) % n_z)
-
-    def weights_out(zz):
-        for k in range(1, n_tm):
-            w_peer(k, zz, tm).start()
-
-    @pl.when(inner)
-    def _():
-        others(weights_out)
 
     for way in (0, 1):
         here = 2 - way

time: 130 us -> 130 us (level)
  no operation moved by 1% of the time
where the time goes in v2:
time: 130 us; the launch traced here: 129 us
  Pallas kernels  127 us (98%)
  local copies, waits for them, and re-layouts  2.36 us (2%)
    pallas_call x1, Pallas kernels, fused(): pl.pallas_call(functools.partial(fused_kernel, n_tm, n_z, frame), out_sha...  127 us

profile of v2, /device:TPU:5, one launch (start us, length us, event | category | flops | bytes accessed | tf_op | source)
XLA Modules:
  0.0 129.5 jit_solution(2325801329204406155)
XLA Ops:
  0.0 127.1 %shard_map.64 = bf16[192,3072]{1,0:T(8,128)(2,1)} custom-call(bf16[192,3072]{1,0:T(8,128)(2,1)} %bitcast.8, bf16[3072,384]{1,0:T(8,128)(2,1)} %bitcast.7, bf16[128,3072]{1,0:T(8,128)(2,1)} %bitcast.9, f32[1,128]{1,0:T(1,128)} %bitcast.10, f32[1,128]{1,0:T(1,128)} %bitcast.11, s32[1,1536]{1,0:T(1,128)} %perm_ref.1), custom_call_target="tpu_custom_call" | custom-call | tf_op jit(solution)/shard_map/pallas_call | solution.py:483
  127.1 2.4 %copy.8 = bf16[1,192,3072]{2,1,0:T(8,128)(2,1)} copy(bf16[1,192,3072]{2,1,0:T(8,128)(2,1)} %bitcast.6) | data formatting | bytes 2359296
